TPU v7x, 32 devices: a whole 2x2x4 slice. The times are simulated.
32 devices in a mesh: user: 4 (over x, core), item: 8 (over z, y).
Axes of the slice: x: 2, y: 2, z: 4, core: 2. Of those that a mesh axis runs over, the one named last changes fastest.
Arguments:
- user_factors: float32 [8192, 256], P(('user', 'item')), may hold values from -6 to 6
- item_factors: bfloat16 [32768, 256], P('item')
- head_ids: int32 [8], replicated, may hold values from 0 to 127, as said below
- tail_ids: int32 [32, 16], P(('user', 'item')), may hold values from 0 to 127, as said below
- head_counts: int32 [32, 8, 256, 256], P(('user', 'item')), may hold values from 0 to 7
- tail_counts: int32 [32, 16, 256, 256], P(('user', 'item')), may hold values from 0 to 7
Outputs:
- new_factors: float32 [8192, 256], P(('user', 'item'))
- residual: float32 [8192, 256], P(('user', 'item'))
Inputs may be any that keep to these rules, and one draw needn't show every extreme that they name: `head_ids`: 8 distinct block numbers, among them 0 and 127. `tail_ids`: each row holds distinct block numbers; at most 4 of a row fall in the range of one index of item (blocks o * 16 to (o + 1) * 16 - 1), and one range, the same for every row, holds exactly 4 of every row.
All inputs are finite; a program needn't handle non-finite values.
Results may differ from a plain program's by a relative error of at most 0.0055.
Values may be sent and summed in bfloat16 or wider, within the bound.
A program may use at most 128 MiB of HBM per device.

v0:
```python
import jax
import jax.numpy as jnp
from jax import lax
from jax.sharding import PartitionSpec as P

ITERS = 2


conf_alpha = 4.0
ridge_term = 0.1
epsilon = 1e-06


def apply_operator(vector, gram_matrix, item_tiles, weights):
    rounded = vector.astype(jnp.bfloat16)
    scores = jnp.einsum("uf,kif->kui", rounded, item_tiles, preferred_element_type=jnp.float32)
    scaled = (scores * weights).astype(jnp.bfloat16)
    data_term = jnp.einsum("kui,kif->uf", scaled, item_tiles, preferred_element_type=jnp.float32)
    gram_term = jnp.dot(vector, gram_matrix, precision=lax.Precision.HIGHEST)
    return gram_term + ridge_term * vector + data_term


def solve_block(start_vec, gram_matrix, item_tiles, counts):
    count_float = counts.astype(jnp.float32)
    weights = (conf_alpha * count_float).astype(jnp.bfloat16)
    rated_weight = jnp.where(counts > 0, 1.0 + conf_alpha * count_float, 0.0).astype(jnp.bfloat16)
    rhs = jnp.einsum("kui,kif->uf", rated_weight, item_tiles, preferred_element_type=jnp.float32)
    solution = start_vec
    residual = rhs - apply_operator(solution, gram_matrix, item_tiles, weights)
    direction = residual
    norm_now = jnp.sum(residual * residual, axis=1, keepdims=True)
    for turn_index in range(ITERS):
        image_vec = apply_operator(direction, gram_matrix, item_tiles, weights)
        step_size = norm_now / (jnp.sum(direction * image_vec, axis=1, keepdims=True) + epsilon)
        solution = solution + step_size * direction
        residual = residual - step_size * image_vec
        if turn_index + 1 < ITERS:
            norm_next = jnp.sum(residual * residual, axis=1, keepdims=True)
            direction = residual + norm_next / (norm_now + epsilon) * direction
            norm_now = norm_next
    return (solution, residual)


def local(user_factors, item_factors, head_ids, tail_ids, head_counts, tail_counts):
    item_count = lax.axis_size("item")
    user_count = lax.axis_size("user")
    block_size = head_counts.shape[-1]
    rank_width = item_factors.shape[1]
    shard_blocks = item_factors.shape[0] // block_size
    blocks = item_factors.reshape(shard_blocks, block_size, rank_width)
    my_item = lax.axis_index("item")
    contract = (((0,), (0,)), ((), ()))
    slice_rows = item_factors.shape[0] // user_count
    rows_part = lax.dynamic_slice_in_dim(
        item_factors, lax.axis_index("user") * slice_rows, slice_rows, 0
    )
    local_gram = lax.dot_general(rows_part, rows_part, contract, preferred_element_type=jnp.float32)
    gram_matrix = lax.psum(local_gram, ("user", "item"))
    head_owner = head_ids // shard_blocks
    head_local = head_ids % shard_blocks
    owned = head_owner == my_item
    picked = jnp.where(owned[:, None, None], blocks[head_local], jnp.zeros((), jnp.bfloat16))
    head_rows = lax.psum(picked, "item").astype(jnp.float32).astype(jnp.bfloat16)
    wanted = tail_ids.reshape(-1)
    length = wanted.shape[0]
    capacity = 2 * length // item_count
    owner_of = wanted // shard_blocks
    local_of = wanted % shard_blocks
    same_owner = owner_of[:, None] == owner_of[None, :]
    positions = jnp.arange(length, dtype=jnp.int32)
    earlier = positions[:, None] > positions[None, :]
    place_index = jnp.sum((same_owner & earlier).astype(jnp.int32), axis=1)
    slot_index = owner_of * capacity + place_index
    slot_table = slot_index[:, None] == jnp.arange(item_count * capacity, dtype=jnp.int32)[None, :]
    requests = jnp.sum(jnp.where(slot_table, local_of[:, None], 0), axis=0)
    requests = requests.reshape(item_count, capacity)
    served = blocks[lax.all_to_all(requests, "item", split_axis=0, concat_axis=0, tiled=True)]
    arrived_tail = lax.all_to_all(served, "item", split_axis=0, concat_axis=0, tiled=True)
    tail_rows = arrived_tail.reshape(item_count * capacity, block_size, rank_width)[slot_index]
    local_blocks = tail_ids.shape[0]
    tail_tiles = tail_rows.reshape(local_blocks, tail_ids.shape[1], block_size, rank_width)
    start_blocks = user_factors.reshape(local_blocks, block_size, rank_width)

    def one_block(block_args):
        start_vec, tail_part_rows, head_part, tail_part = block_args
        item_tiles = jnp.concatenate([head_rows, tail_part_rows], axis=0)
        counts = jnp.concatenate([head_part, tail_part], axis=0)
        return solve_block(start_vec, gram_matrix, item_tiles, counts)

    solution, residual = lax.map(one_block, (start_blocks, tail_tiles, head_counts, tail_counts))
    return (
        solution.reshape(local_blocks * block_size, rank_width),
        residual.reshape(local_blocks * block_size, rank_width),
    )


def solution(mesh):
    return jax.shard_map(
        local,
        mesh=mesh,
        in_specs=(
            P(("user", "item"), None),
            P("item", None),
            P(),
            P(("user", "item"), None),
            P(("user", "item"), None, None, None),
            P(("user", "item"), None, None, None),
        ),
        out_specs=(P(("user", "item"), None), P(("user", "item"), None)),
        check_vma=False,
    )
```

profile of v0, /device:TPU:5, one launch (start us, length us, event | category | flops | bytes accessed | tf_op | source)
XLA Modules:
  0.0 336.1 jit_solution(14592316701948671796)
XLA Ops:
  7.2 0.0 copy-start
  7.2 0.8 and_select_fusion.3
  8.0 0.7 fusion.48
  8.7 0.2 convert_reduce_fusion
  8.8 0.1 select_reduce_fusion
  8.9 0.1 all_to_all.11
  9.0 9.7 %all_to_all.17 = s32[8,1,4]{2,1,0:T(1,128)S(1)} all-to-all(s32[8,1,4]{2,1,0:T(1,128)S(1)} %bitcast.103), channel_id=1, replica_groups=mesh['user'=4,'item'=8] {'item'}, dimensions={0} | all-to-all | bytes 256 | tf_op jit(solution)/shard_map/all_to_all | solution.py:77
  18.7 0.1 copy.46
  18.8 0.1 copy.47
  18.9 0.1 reshape.226
  19.0 0.0 copy-done
  19.0 2.8 gather_fusion.1
  21.8 0.0 copy-start.3
  21.8 5.7 %all-to-all-start.1 = ((bf16[8,4,256,256]{3,2,1,0:T(8,128)(2,1)}), bf16[8,4,256,256]{3,2,1,0:T(8,128)(2,1)}, u32[]{:S(2)}, u32[]{:S(2)}) async-start(bf16[8,4,256,256]{3,2,1,0:T(8,128)(2,1)} %bitcast.94), calls=%async_computation.1 | async-start | bytes 8388608 | tf_op jit(solution)/shard_map/all_to_all | solution.py:78
  27.5 0.0 all-reduce.3.cloned.1.call-start
  27.5 0.0 copy-done.3
  27.6 1.6 gather_fusion
  29.1 1.5 copy.44
  30.7 1.1 broadcast_select_fusion
  31.8 0.0 all-reduce.3.cloned.1.call-update
  31.8 0.0 all-reduce.5.cloned.1.call-start
  31.9 1.0 fusion.32
  32.9 0.0 all-reduce.5.cloned.1.call-update
  32.9 5.4 %copy.43 = s32[1,16,256,256]{2,3,1,0:T(8,128)} copy(s32[1,16,256,256]{3,2,1,0:T(8,128)} %param.11) | data formatting | bytes 8388608 | tf_op args[5]
  38.3 0.0 copy-start.2
  38.3 0.0 copy-start.4
  38.3 3.0 copy.42
  41.3 0.0 copy-done.2
  41.3 0.1 copy.56
  41.4 0.0 copy-done.4
  41.4 93.3 %all-to-all-done.1 = bf16[8,4,256,256]{3,2,1,0:T(8,128)(2,1)} async-done(((bf16[8,4,256,256]{3,2,1,0:T(8,128)(2,1)}), bf16[8,4,256,256]{3,2,1,0:T(8,128)(2,1)}, u32[]{:S(2)}, u32[]{:S(2)}) %all-to-all-start.1) | async-done | bytes 4194336 | tf_op jit(solution)/shard_map/all_to_all | solution.py:78
  134.7 4.3 %gather_fusion.2 = bf16[16,256,256]{2,1,0:T(8,128)(2,1)} fusion(bf16[32,256,256]{2,1,0:T(8,128)(2,1)} %bitcast.8, s32[1024]{0:T(1024)S(1)} %pad_clamp_fusion), kind=kCustom, calls=%fused_computation.2 | custom fusion | bytes 4194368 | tf_op jit(solution)/shard_map/gather | solution.py:79
  139.0 3.9 %copy.48 = bf16[16,256,256]{1,2,0:T(8,128)(2,1)} copy(bf16[16,256,256]{2,1,0:T(8,128)(2,1)} %gather_fusion.2) | data formatting | bytes 4194304 | tf_op jit(solution)/shard_map/gather | solution.py:79
  142.9 31.9 %all-reduce.3.cloned.1.call-done = bf16[8,256,256]{1,2,0:T(8,128)(2,1)} async-done(((bf16[8,256,256]{1,2,0:T(8,128)(2,1)}), bf16[8,256,256]{1,2,0:T(8,128)(2,1)}) %all-reduce.3.cloned.1.call-update) | async-done | bytes 1048592 | tf_op jit(solution)/shard_map/psum | solution.py:63
  174.9 6.7 %fusion.23 = f32[256,256]{0,1:T(8,128)S(1)} fusion(f32[256,256]{1,0:T(8,128)S(1)} %copy-done.2, bf16[16,256,256]{1,2,0:T(8,128)(2,1)} %copy.48, bf16[8,256,256]{1,2,0:T(8,128)(2,1)} %all-reduce.3.cloned.1.call-done, s32[16,256,256]{1,2,0:T(8,128)} %bitcast.95, s32[8,256,256]{1,2,0:T(8,128)} %bitcast.99), kind=kOutput, calls=%fused_computation.30 | convolution fusion | flops 1624834048 | bytes 9961472 | tf_op jit(solution)/shard_map/while/body/eval_jaxpr/kui,kif->uf/dot_general | solution.py:18
  181.5 5.1 %fusion.17 = f32[256,256]{0,1:T(8,128)S(1)} fusion(s32[16,256,256]{1,2,0:T(8,128)} %bitcast.96, s32[8,256,256]{1,2,0:T(8,128)} %bitcast.100, bf16[16,256,256]{1,2,0:T(8,128)(2,1)} %copy.48, bf16[8,256,256]{1,2,0:T(8,128)(2,1)} %all-reduce.3.cloned.1.call-done), kind=kOutput, calls=%fused_computation.21 | convolution fusion | flops 817889280 | bytes 9699328 | tf_op jit(solution)/shard_map/while/body/eval_jaxpr/kui,kif->uf/dot_general | solution.py:27
  186.6 119.6 %all-reduce.5.cloned.1.call-done = f32[256,256]{1,0:T(8,128)} async-done(((f32[256,256]{1,0:T(8,128)}), f32[256,256]{1,0:T(8,128)}) %all-reduce.5.cloned.1.call-update) | async-done | bytes 262160 | tf_op jit(solution)/shard_map/psum | solution.py:58
  306.2 1.5 fusion.22
  307.8 0.0 copy-start.1
  307.8 7.5 %fusion.26 = f32[256,256]{0,1:T(8,128)S(1)} fusion(f32[256,256]{0,1:T(8,128)S(1)} %fusion.22, bf16[16,256,256]{1,2,0:T(8,128)(2,1)} %copy.48, bf16[8,256,256]{1,2,0:T(8,128)(2,1)} %all-reduce.3.cloned.1.call-done, s32[16,256,256]{1,2,0:T(8,128)} %bitcast.97, s32[8,256,256]{1,2,0:T(8,128)} %bitcast.101), kind=kOutput, calls=%fused_computation.31 | convolution fusion | flops 1624834048 | bytes 9961472 | tf_op jit(solution)/shard_map/while/body/eval_jaxpr/kui,kif->uf/dot_general | solution.py:18
  315.3 0.0 copy-done.1
  315.3 0.6 multiply_reduce_fusion.2
  315.9 0.1 multiply_reduce_fusion.1
  316.1 8.2 %fusion.29 = f32[256,256]{0,1:T(8,128)} fusion(f32[256,256]{0,1:T(8,128)S(1)} %multiply_add_fusion.1, bf16[16,256,256]{1,2,0:T(8,128)(2,1)} %copy.48, bf16[8,256,256]{1,2,0:T(8,128)(2,1)} %all-reduce.3.cloned.1.call-done, s32[16,256,256]{1,2,0:T(8,128)} %bitcast.98, s32[8,256,256]{1,2,0:T(8,128)} %bitcast.102), kind=kOutput, calls=%fused_computation.32 | convolution fusion | flops 1624834048 | bytes 9961472 | tf_op jit(solution)/shard_map/while/body/eval_jaxpr/kui,kif->uf/dot_general | solution.py:18
  324.3 1.6 multiply_reduce_fusion
  325.8 0.8 multiply_subtract_fusion
  326.6 1.8 copy.60
  328.4 0.8 copy.61
  (12 shorter events, 0.1 us)
Async XLA Ops:
  7.2 11.8 %copy-start = (bf16[4096,256]{1,0:T(8,128)(2,1)S(1)}, bf16[4096,256]{1,0:T(8,128)(2,1)}, u32[]{:S(2)}) copy-start(bf16[4096,256]{1,0:T(8,128)(2,1)} %param.7) | copy-start | bytes 6291460
  21.8 5.7 %copy-start.3 = (s32[8]{0:T(128)S(1)}, s32[8]{0:T(128)}, u32[]{:S(2)}) copy-start(s32[8]{0:T(128)} %param.8) | copy-start | bytes 100
  21.8 113.0 %all-to-all-start.1 = ((bf16[8,4,256,256]{3,2,1,0:T(8,128)(2,1)}), bf16[8,4,256,256]{3,2,1,0:T(8,128)(2,1)}, u32[]{:S(2)}, u32[]{:S(2)}) async-start(bf16[8,4,256,256]{3,2,1,0:T(8,128)(2,1)} %bitcast.94), calls=%async_computation.1 | async-start | bytes 8388608 | tf_op jit(solution)/shard_map/all_to_all | solution.py:78
  27.5 147.3 %all-reduce.3.cloned.1.call-start = ((), (), s32[]{:S(2)}) async-start(), calls=%async_computation.2 | async-start | bytes 2097152 | tf_op jit(solution)/shard_map/psum | solution.py:63
  31.8 274.4 %all-reduce.5.cloned.1.call-start = ((), (), s32[]{:S(2)}) async-start(), calls=%async_computation.3 | async-start | bytes 524288 | tf_op jit(solution)/shard_map/psum | solution.py:58
  38.3 3.0 copy-start.2
  38.3 3.1 copy-start.4
  307.8 7.5 %copy-start.1 = (f32[256,256]{1,0:T(8,128)S(1)}, f32[256,256]{1,0:T(8,128)}, u32[]{:S(2)}) copy-start(f32[256,256]{1,0:T(8,128)} %all-reduce.5.cloned.1.call-done) | copy-start | bytes 786436
Sparse Core Ops, SparseCore 0:
  31.9 142.8 all-reduce.2
  181.9 124.3 all-reduce.4
where the time goes:
time: 339 us; the launch traced here: 336 us
  waiting for transfers between devices  245 us (72%)
  matrix products  32.2 us (9%)
  local copies, waits for them, and re-layouts  25.5 us (8%)
  between operations  14.2 us (4%)
  blocking collectives  9.69 us (3%)
  starting transfers between devices  5.79 us (2%)
  other arithmetic  3.89 us (1%)
    psum x1, waiting for transfers between devices, local(): gram_matrix = lax.psum(local_gram, ('user', 'item'))  120 us
    all_to_all x1, waiting for transfers between devices, local(): lax.all_to_all(served, 'item', split_axis=0, concat_axis=0, tiled=True)  93.3 us
    psum x1, waiting for transfers between devices, local(): lax.psum(picked, 'item').astype(jnp.float32).astype(jnp.bfloat16)  31.9 us
    dot_general x3, matrix products, apply_operator(): jnp.einsum('kui,kif->uf', scaled, item_tiles, preferred_element_type=jnp....  22.4 us
    unnamed x15, local copies, waits for them, and re-layouts  11.1 us
    all_to_all x1, blocking collectives, local(): lax.all_to_all(requests, 'item', split_axis=0, concat_axis=0, tiled=True)  9.69 us
    gather x2, local copies, waits for them, and re-layouts, local(): arrived_tail.reshape(item_count * capacity, block_size, rank_width)  8.2 us
  transfers between devices with their start and end apart: 3, of which 3 were waited for; matrix products, arithmetic and copies ran while one was open for 10% of the time, Pallas kernels for 0%

commit v1 on v0

--- a/solution.py
+++ b/solution.py
@@ -1,6 +1,8 @@
 import jax
 import jax.numpy as jnp
 from jax import lax
+from jax.experimental import pallas as pl
+from jax.experimental.pallas import tpu as pltpu
 from jax.sharding import PartitionSpec as P
 
 ITERS = 2
@@ -41,6 +43,12 @@
     return (solution, residual)
 
 
+def take_blocks(blocks, ids):
+    return jnp.stack(
+        [lax.dynamic_index_in_dim(blocks, ids[k], 0, keepdims=False) for k in range(ids.shape[0])]
+    )
+
+
 def local(user_factors, item_factors, head_ids, tail_ids, head_counts, tail_counts):
     item_count = lax.axis_size("item")
     user_count = lax.axis_size("user")
@@ -59,7 +67,7 @@
     head_owner = head_ids // shard_blocks
     head_local = head_ids % shard_blocks
     owned = head_owner == my_item
-    picked = jnp.where(owned[:, None, None], blocks[head_local], jnp.zeros((), jnp.bfloat16))
+    picked = jnp.where(owned[:, None, None], take_blocks(blocks, head_local), jnp.zeros((), jnp.bfloat16))
     head_rows = lax.psum(picked, "item").astype(jnp.float32).astype(jnp.bfloat16)
     wanted = tail_ids.reshape(-1)
     length = wanted.shape[0]
@@ -74,9 +82,12 @@
     slot_table = slot_index[:, None] == jnp.arange(item_count * capacity, dtype=jnp.int32)[None, :]
     requests = jnp.sum(jnp.where(slot_table, local_of[:, None], 0), axis=0)
     requests = requests.reshape(item_count, capacity)
-    served = blocks[lax.all_to_all(requests, "item", split_axis=0, concat_axis=0, tiled=True)]
+    asked = lax.all_to_all(requests, "item", split_axis=0, concat_axis=0, tiled=True)
+    served = take_blocks(blocks, asked.reshape(-1)).reshape(item_count, capacity, block_size, rank_width)
     arrived_tail = lax.all_to_all(served, "item", split_axis=0, concat_axis=0, tiled=True)
-    tail_rows = arrived_tail.reshape(item_count * capacity, block_size, rank_width)[slot_index]
+    tail_rows = take_blocks(
+        arrived_tail.reshape(item_count * capacity, block_size, rank_width), slot_index
+    )
     local_blocks = tail_ids.shape[0]
     tail_tiles = tail_rows.reshape(local_blocks, tail_ids.shape[1], block_size, rank_width)
     start_blocks = user_factors.reshape(local_blocks, block_size, rank_width)
@@ -94,9 +105,262 @@
     )
 
 
+PARTS = 2
+STEPS = (1, 3, 2)
+
+
+def gather_kernel(shard, out, send_sem, recv_sem, own_sem):
+    user, item = lax.axis_index("user"), lax.axis_index("item")
+    x, c = user // 2, user % 2
+    z, y = item // 2, item % 2
+    rows = shard.shape[1] // PARTS
+
+    def dev(x_at, y_at, z_at, c_at):
+        return (x_at * 2 + c_at, z_at * 2 + y_at)
+
+    side_x, side_y, side_c = dev(1 - x, y, z, c), dev(x, 1 - y, z, c), dev(x, y, z, 1 - c)
+    barrier = pltpu.get_barrier_semaphore()
+    for other in [side_x, side_y, side_c] + [dev(x, y, (z + r) % 4, c) for r in STEPS]:
+        pl.semaphore_signal(barrier, inc=1, device_id=other, device_id_type=pl.DeviceIdType.MESH)
+    pl.semaphore_wait(barrier, 6)
+
+    def place(z_at, y_at, x_at, part):
+        return out.at[z_at * 2 + y_at, x_at * 2 + c, pl.ds(part * rows, rows)]
+
+    slots = {}
+
+    def slot(name):
+        return slots.setdefault(name, len(slots))
+
+    def copy(name, source, target, device):
+        return pltpu.make_async_remote_copy(
+            src_ref=source,
+            dst_ref=target,
+            send_sem=send_sem.at[slot(name)],
+            recv_sem=recv_sem.at[slot(name)],
+            device_id=device,
+            device_id_type=pl.DeviceIdType.MESH,
+        )
+
+    started = []
+
+    def send(name, source, target, device):
+        made = copy(name, source, target, device)
+        made.start()
+        started.append(made)
+
+    def arrive(name, target):
+        copy(name, target, target, side_c).wait_recv()
+
+    def pass_on(name, target):
+        send(("c",) + name, target, target, side_c)
+
+    own = pltpu.make_async_copy(shard, out.at[item], own_sem)
+    own.start()
+    for part in range(PARTS):
+        piece = shard.at[x * 2 + c, pl.ds(part * rows, rows)]
+        far = shard.at[(1 - x) * 2 + c, pl.ds(part * rows, rows)]
+        for r in STEPS:
+            send(("z", r, part), piece, place(z, y, x, part), dev(x, y, (z + r) % 4, c))
+        send(("y", 0, part), piece, place(z, y, x, part), side_y)
+        send(("d", 0, part), far, place(z, y, 1 - x, part), side_y)
+    landed = []
+
+    def take(name, target):
+        arrive(name, target)
+        pass_on(name, target)
+        landed.append((("c",) + name, name))
+
+    for part in range(PARTS):
+        for r in STEPS:
+            here = place((z + 4 - r) % 4, y, x, part)
+            arrive(("z", r, part), here)
+            send(("x", r, part), here, here, side_x)
+            send(("y", r, part), here, here, side_y)
+            pass_on(("z", r, part), here)
+        take(("y", 0, part), place(z, 1 - y, x, part))
+        take(("d", 0, part), place(z, 1 - y, 1 - x, part))
+    for part in range(PARTS):
+        for r in STEPS:
+            plane = (z + 4 - r) % 4
+            from_x = place(plane, y, 1 - x, part)
+            from_y = place(plane, 1 - y, x, part)
+            by_x = r == 1 or (r == 2 and part % 2 == 0) or (r == 3 and part % 2 == 0)
+            arrive(("x", r, part), from_x)
+            if not by_x:
+                send(("d", r, part), from_x, from_x, side_y)
+            pass_on(("x", r, part), from_x)
+            arrive(("y", r, part), from_y)
+            if by_x:
+                send(("d", r, part), from_y, from_y, side_x)
+            pass_on(("y", r, part), from_y)
+    for part in range(PARTS):
+        for r in STEPS:
+            take(("d", r, part), place((z + 4 - r) % 4, 1 - y, 1 - x, part))
+
+    def other_core(z_at, y_at, x_at, part):
+        return out.at[z_at * 2 + y_at, x_at * 2 + 1 - c, pl.ds(part * rows, rows)]
+
+    for part in range(PARTS):
+        arrive(("c", "y", 0, part), other_core(z, 1 - y, x, part))
+        arrive(("c", "d", 0, part), other_core(z, 1 - y, 1 - x, part))
+        for r in STEPS:
+            plane = (z + 4 - r) % 4
+            arrive(("c", "z", r, part), other_core(plane, y, x, part))
+            arrive(("c", "x", r, part), other_core(plane, y, 1 - x, part))
+            arrive(("c", "y", r, part), other_core(plane, 1 - y, x, part))
+            arrive(("c", "d", r, part), other_core(plane, 1 - y, 1 - x, part))
+    for made in started:
+        made.wait_send()
+    own.wait()
+
+
+COPIES = PARTS * (3 + 3 + 4 + 4 + 14)
+
+
+def gather_all(item_factors, item_count):
+    rows, width = item_factors.shape
+    shard = item_factors.reshape(4, rows // 4, width)
+    return pl.pallas_call(
+        gather_kernel,
+        out_shape=jax.ShapeDtypeStruct((item_count, 4, rows // 4, width), item_factors.dtype),
+        in_specs=[pl.BlockSpec(memory_space=pl.ANY)],
+        out_specs=pl.BlockSpec(memory_space=pl.ANY),
+        scratch_shapes=[
+            pltpu.SemaphoreType.DMA((COPIES,)),
+            pltpu.SemaphoreType.DMA((COPIES,)),
+            pltpu.SemaphoreType.DMA,
+        ],
+        compiler_params=pltpu.CompilerParams(collective_id=0, has_side_effects=True),
+    )(shard)
+
+
+GROUP = 4
+
+
+def solve_kernel(
+    head_ids, tail_ids, start, gram, head_counts, tail_counts, items, out, residual_out, tiles, weights, acc, sem
+):
+    head_count, tail_count = head_counts.shape[0], tail_counts.shape[0]
+    total = head_count + tail_count
+    size, width = tiles.shape[1], tiles.shape[2]
+
+    def fetch(k):
+        block = head_ids[k] if k < head_count else tail_ids[k - head_count]
+        return pltpu.make_async_copy(items.at[block], tiles.at[k], sem.at[k])
+
+    for k in range(total):
+        fetch(k).start()
+    last = (((1,), (1,)), ((), ()))
+
+    def group_tiles(g):
+        return tiles[pl.ds(g * GROUP, GROUP)].reshape(GROUP * size, width)
+
+    def data_part(rounded, rows, weight):
+        scores = lax.dot_general(rounded, rows, last, preferred_element_type=jnp.float32)
+        scaled = (scores * weight.astype(jnp.float32)).astype(jnp.bfloat16)
+        return jnp.dot(scaled, rows, preferred_element_type=jnp.float32)
+
+    def dense_part(vector):
+        image = jnp.dot(
+            vector, gram[...], precision=lax.Precision.HIGHEST, preferred_element_type=jnp.float32
+        )
+        return image + ridge_term * vector
+
+    start_vec = start[...]
+    acc[...] = -dense_part(start_vec)
+    rounded_start = start_vec.astype(jnp.bfloat16)
+    for k in range(total):
+        fetch(k).wait()
+
+    def first(counts, base):
+        def body(g, carry):
+            weight_list, rated_list = [], []
+            for k in range(GROUP):
+                count = counts[g * GROUP + k].astype(jnp.float32)
+                weight = conf_alpha * count
+                weight_list.append(weight.astype(jnp.bfloat16))
+                rated_list.append(jnp.where(count > 0, 1.0 + weight, 0.0).astype(jnp.bfloat16))
+            weight = jnp.concatenate(weight_list, axis=1)
+            rated = jnp.concatenate(rated_list, axis=1)
+            weights[base + g] = weight
+            rows = group_tiles(base + g)
+            acc[...] += jnp.dot(rated, rows, preferred_element_type=jnp.float32) - data_part(
+                rounded_start, rows, weight
+            )
+            return carry
+
+        lax.fori_loop(0, counts.shape[0] // GROUP, body, 0)
+
+    first(head_counts, 0)
+    first(tail_counts, head_count // GROUP)
+
+    def apply(vector):
+        acc[...] = dense_part(vector)
+        rounded = vector.astype(jnp.bfloat16)
+
+        def body(g, carry):
+            acc[...] += data_part(rounded, group_tiles(g), weights[g])
+            return carry
+
+        lax.fori_loop(0, total // GROUP, body, 0)
+        return acc[...]
+
+    solution = start_vec
+    residual = acc[...]
+    direction = residual
+    norm_now = jnp.sum(residual * residual, axis=1, keepdims=True)
+    for turn_index in range(ITERS):
+        image_vec = apply(direction)
+        step_size = norm_now / (jnp.sum(direction * image_vec, axis=1, keepdims=True) + epsilon)
+        solution = solution + step_size * direction
+        residual = residual - step_size * image_vec
+        if turn_index + 1 < ITERS:
+            norm_next = jnp.sum(residual * residual, axis=1, keepdims=True)
+            direction = residual + norm_next / (norm_now + epsilon) * direction
+            norm_now = norm_next
+    out[...] = solution
+    residual_out[...] = residual
+
+
+def local_gathered(user_factors, item_factors, head_ids, tail_ids, head_counts, tail_counts):
+    size, width = head_counts.shape[-1], item_factors.shape[1]
+    items = gather_all(item_factors, lax.axis_size("item"))
+    flat = items.reshape(-1, width)
+    gram_matrix = lax.dot_general(
+        flat, flat, (((0,), (0,)), ((), ())), preferred_element_type=jnp.float32
+    )
+    total = head_counts.shape[1] + tail_counts.shape[1]
+    smem = pl.BlockSpec(memory_space=pltpu.SMEM)
+    vmem = pl.BlockSpec(memory_space=pltpu.VMEM)
+    shape = jax.ShapeDtypeStruct(user_factors.shape, jnp.float32)
+    return pl.pallas_call(
+        solve_kernel,
+        out_shape=(shape, shape),
+        in_specs=[smem, smem, vmem, vmem, vmem, vmem, pl.BlockSpec(memory_space=pl.ANY)],
+        out_specs=(vmem, vmem),
+        scratch_shapes=[
+            pltpu.VMEM((total, size, width), jnp.bfloat16),
+            pltpu.VMEM((total // GROUP, size, GROUP * size), jnp.bfloat16),
+            pltpu.VMEM((size, width), jnp.float32),
+            pltpu.SemaphoreType.DMA((total,)),
+        ],
+        compiler_params=pltpu.CompilerParams(vmem_limit_bytes=40 * 1024 * 1024),
+    )(
+        head_ids,
+        tail_ids.reshape(-1),
+        user_factors,
+        gram_matrix,
+        head_counts[0],
+        tail_counts[0],
+        items.reshape(-1, size, width),
+    )
+
+
 def solution(mesh):
+    small = mesh.shape["user"] == 4 and mesh.shape["item"] == 8
     return jax.shard_map(
-        local,
+        local_gathered if small else local,
         mesh=mesh,
         in_specs=(
             P(("user", "item"), None),

time: 339 us -> 119 us (0.35)
  the two profiles are of different devices: /device:TPU:5 before, /device:TPU:17 now
where the time goes in v1:
time: 119 us
  Pallas kernels  104 us (87%)
  matrix products  14.2 us (12%)
    pallas_call x1, Pallas kernels, gather_all(): pl.pallas_call(gather_kernel, out_shape=jax.ShapeDtypeStruct((item_count,...  88 us
    pallas_call x1, Pallas kernels, local_gathered(): pl.pallas_call(solve_kernel, out_shape=(shape, shape), in_specs=[smem, sm...  15.8 us
    dot_general x1, matrix products, local_gathered(): lax.dot_general(flat, flat, (((0,), (0,)), ((), ())), preferred_element_t...  14.2 us

profile of v1, /device:TPU:17, one launch (start us, length us, event | category | flops | bytes accessed | tf_op | source)
XLA Modules:
  0.0 118.8 jit_solution(3922946142685546506)
XLA Ops:
  0.6 88.0 %shard_map.77 = bf16[8,4,1024,256]{3,2,1,0:T(8,128)(2,1)} custom-call(bf16[4,1024,256]{2,1,0:T(8,128)(2,1)} %bitcast.15), custom_call_target="tpu_custom_call" | custom-call | tf_op jit(solution)/shard_map/pallas_call | solution.py:224
  88.6 0.0 copy-start
  88.7 0.0 copy-start.1
  88.7 0.0 copy-start.2
  88.7 0.0 copy-start.3
  88.7 0.0 copy-start.4
  88.7 14.2 %convolution_bitcast_fusion.gram = f32[256,256]{1,0:T(8,128)S(1)} fusion(bf16[8,4,1024,256]{3,2,1,0:T(8,128)(2,1)} %shard_map.77), kind=kOutput, calls=%fused_computation | convolution fusion | flops 4294967296 | bytes 17039360 | tf_op jit(solution)/shard_map/dot_general | solution.py:330
  102.9 0.0 copy-done
  102.9 0.0 copy-done.1
  102.9 0.0 copy-done.2
  103.0 0.0 copy-done.3
  103.0 0.0 copy-done.4
  103.0 15.8 %shard_map.78 = (f32[256,256]{1,0:T(8,128)}, f32[256,256]{1,0:T(8,128)}) custom-call(s32[8]{0:T(128)S(1)} %copy-done.3, s32[16]{0:T(128)S(1)} %bitcast.13, f32[256,256]{1,0:T(8,128)S(1)} %copy-done.2, f32[256,256]{1,0:T(8,128)S(1)} %convolution_bitcast_fusion.gram, s32[8,256,256]{2,1,0:T(8,128)S(1)} %bitcast.12, s32[16,256,256]{2,1,0:T(8,128)S(1)} %bitcast.11, ...), custom_call_target="tpu_custom_call" | custom-call | tf_op jit(solution)/shard_map/pallas_call | solution.py:337
Async XLA Ops:
  88.6 14.3 %copy-start = (s32[1,16,256,256]{3,2,1,0:T(8,128)S(1)}, s32[1,16,256,256]{3,2,1,0:T(8,128)}, u32[]{:S(2)}) copy-start(s32[1,16,256,256]{3,2,1,0:T(8,128)} %param.11) | copy-start | bytes 12582916
  88.7 14.3 %copy-start.1 = (s32[1,8,256,256]{3,2,1,0:T(8,128)S(1)}, s32[1,8,256,256]{3,2,1,0:T(8,128)}, u32[]{:S(2)}) copy-start(s32[1,8,256,256]{3,2,1,0:T(8,128)} %param.10) | copy-start | bytes 6291460
  88.7 14.3 %copy-start.2 = (f32[256,256]{1,0:T(8,128)S(1)}, f32[256,256]{1,0:T(8,128)}, u32[]{:S(2)}) copy-start(f32[256,256]{1,0:T(8,128)} %start.1) | copy-start | bytes 786436
  88.7 14.3 %copy-start.3 = (s32[8]{0:T(128)S(1)}, s32[8]{0:T(128)}, u32[]{:S(2)}) copy-start(s32[8]{0:T(128)} %head_ids.1) | copy-start | bytes 100
  88.7 14.3 %copy-start.4 = (s32[1,16]{1,0:T(1,128)S(1)}, s32[1,16]{1,0:T(1,128)}, u32[]{:S(2)}) copy-start(s32[1,16]{1,0:T(1,128)} %param.9) | copy-start | bytes 196

commit v2 on v1

--- a/solution.py
+++ b/solution.py
@@ -105,15 +105,24 @@
     )
 
 
-PARTS = 2
+PARTS = 4
 STEPS = (1, 3, 2)
-
-
-def gather_kernel(shard, out, send_sem, recv_sem, own_sem):
+GROUP = 4
+COPIES = PARTS * (3 + 3 + 4 + 4 + 14) + 1
+
+
+def solve_kernel(
+    head_ids, tail_ids, start, shard, head_counts, tail_counts, out, residual_out,
+    items, head_held, tail_held, weights, rated, gram, gram_other, acc,
+    send_sem, recv_sem, own_sem,
+):
     user, item = lax.axis_index("user"), lax.axis_index("item")
     x, c = user // 2, user % 2
     z, y = item // 2, item % 2
-    rows = shard.shape[1] // PARTS
+    shard_blocks, size, width = shard.shape
+    quarter = shard_blocks // 4
+    run = quarter // PARTS
+    heads, tails = head_counts.shape[0], tail_counts.shape[0]
 
     def dev(x_at, y_at, z_at, c_at):
         return (x_at * 2 + c_at, z_at * 2 + y_at)
@@ -122,10 +131,20 @@
     barrier = pltpu.get_barrier_semaphore()
     for other in [side_x, side_y, side_c] + [dev(x, y, (z + r) % 4, c) for r in STEPS]:
         pl.semaphore_signal(barrier, inc=1, device_id=other, device_id_type=pl.DeviceIdType.MESH)
+    own = pltpu.make_async_copy(shard, items.at[pl.ds(item * shard_blocks, shard_blocks)], own_sem.at[0])
+    head_in = pltpu.make_async_copy(head_counts, head_held, own_sem.at[1])
+    tail_in = pltpu.make_async_copy(tail_counts, tail_held, own_sem.at[2])
+    own.start()
     pl.semaphore_wait(barrier, 6)
 
+    def first_block(z_at, y_at, x_at, part, core):
+        return (z_at * 2 + y_at) * shard_blocks + (x_at * 2 + core) * quarter + part * run
+
     def place(z_at, y_at, x_at, part):
-        return out.at[z_at * 2 + y_at, x_at * 2 + c, pl.ds(part * rows, rows)]
+        return items.at[pl.ds(first_block(z_at, y_at, x_at, part, c), run)]
+
+    def other_core(z_at, y_at, x_at, part):
+        return items.at[pl.ds(first_block(z_at, y_at, x_at, part, 1 - c), run)]
 
     slots = {}
 
@@ -155,23 +174,37 @@
     def pass_on(name, target):
         send(("c",) + name, target, target, side_c)
 
-    own = pltpu.make_async_copy(shard, out.at[item], own_sem)
-    own.start()
+    def take(name, target):
+        arrive(name, target)
+        pass_on(name, target)
+
     for part in range(PARTS):
-        piece = shard.at[x * 2 + c, pl.ds(part * rows, rows)]
-        far = shard.at[(1 - x) * 2 + c, pl.ds(part * rows, rows)]
+        piece = shard.at[pl.ds((x * 2 + c) * quarter + part * run, run)]
+        far = shard.at[pl.ds(((1 - x) * 2 + c) * quarter + part * run, run)]
         for r in STEPS:
             send(("z", r, part), piece, place(z, y, x, part), dev(x, y, (z + r) % 4, c))
         send(("y", 0, part), piece, place(z, y, x, part), side_y)
         send(("d", 0, part), far, place(z, y, 1 - x, part), side_y)
-    landed = []
-
-    def take(name, target):
-        arrive(name, target)
-        pass_on(name, target)
-        landed.append((("c",) + name, name))
-
-    for part in range(PARTS):
+    head_in.start()
+    tail_in.start()
+
+    rows_out = (((0,), (0,)), ((), ()))
+
+    def gram_add(z_at, y_at, x_at, part):
+        first = first_block(z_at, y_at, x_at, part, c)
+        for k in range(run):
+            rows = items[first + k]
+            gram[...] += lax.dot_general(rows, rows, rows_out, preferred_element_type=jnp.float32)
+
+    def gram_planes(places, part):
+        def body(r, carry):
+            for y_at, x_at in places:
+                gram_add((z + 4 - r) % 4, y_at, x_at, part)
+            return carry
+
+        lax.fori_loop(1, 4, body, 0)
+
+    def column_part(part):
         for r in STEPS:
             here = place((z + 4 - r) % 4, y, x, part)
             arrive(("z", r, part), here)
@@ -180,11 +213,11 @@
             pass_on(("z", r, part), here)
         take(("y", 0, part), place(z, 1 - y, x, part))
         take(("d", 0, part), place(z, 1 - y, 1 - x, part))
-    for part in range(PARTS):
+
+    def side_part(part):
         for r in STEPS:
             plane = (z + 4 - r) % 4
-            from_x = place(plane, y, 1 - x, part)
-            from_y = place(plane, 1 - y, x, part)
+            from_x, from_y = place(plane, y, 1 - x, part), place(plane, 1 - y, x, part)
             by_x = r == 1 or (r == 2 and part % 2 == 0) or (r == 3 and part % 2 == 0)
             arrive(("x", r, part), from_x)
             if not by_x:
@@ -194,13 +227,65 @@
             if by_x:
                 send(("d", r, part), from_y, from_y, side_x)
             pass_on(("y", r, part), from_y)
-    for part in range(PARTS):
+
+    def corner_part(part):
         for r in STEPS:
             take(("d", r, part), place((z + 4 - r) % 4, 1 - y, 1 - x, part))
 
-    def other_core(z_at, y_at, x_at, part):
-        return out.at[z_at * 2 + y_at, x_at * 2 + 1 - c, pl.ds(part * rows, rows)]
-
+    def weigh(held, base):
+        def body(g, carry):
+            weight_list, rated_list = [], []
+            for k in range(GROUP):
+                count = held[g * GROUP + k].astype(jnp.float32)
+                weight = conf_alpha * count
+                weight_list.append(weight.astype(jnp.bfloat16))
+                rated_list.append(jnp.where(count > 0, 1.0 + weight, 0.0).astype(jnp.bfloat16))
+            weights[base + g] = jnp.concatenate(weight_list, axis=1)
+            rated[base + g] = jnp.concatenate(rated_list, axis=1)
+            return carry
+
+        lax.fori_loop(0, held.shape[0] // GROUP, body, 0)
+
+    gram[...] = jnp.zeros_like(gram)
+    own.wait()
+    for part in range(PARTS + 2):
+        if part < PARTS:
+            column_part(part)
+        if 1 <= part <= PARTS:
+            side_part(part - 1)
+        if part >= 2:
+            corner_part(part - 2)
+        if part < PARTS:
+            gram_planes([(y, x)], part)
+            for y_at, x_at in ((y, x), (y, 1 - x), (1 - y, x), (1 - y, 1 - x)):
+                gram_add(z, y_at, x_at, part)
+        if 1 <= part <= PARTS:
+            gram_planes([(y, 1 - x), (1 - y, x)], part - 1)
+        if part == 0:
+            head_in.wait()
+            weigh(head_held, 0)
+        if part == 1:
+            tail_in.wait()
+            weigh(tail_held, heads // GROUP)
+        if part >= 2:
+            gram_planes([(1 - y, 1 - x)], part - 2)
+    send(("gram",), gram, gram_other, side_c)
+    arrive(("gram",), gram_other)
+
+    last = (((1,), (1,)), ((), ()))
+
+    def dense_part(vector):
+        image = jnp.dot(
+            vector,
+            gram[...] + gram_other[...],
+            precision=lax.Precision.HIGHEST,
+            preferred_element_type=jnp.float32,
+        )
+        return image + ridge_term * vector
+
+    start_vec = start[...]
+    acc[...] = -dense_part(start_vec)
+    rounded_start = start_vec.astype(jnp.bfloat16)
     for part in range(PARTS):
         arrive(("c", "y", 0, part), other_core(z, 1 - y, x, part))
         arrive(("c", "d", 0, part), other_core(z, 1 - y, 1 - x, part))
@@ -210,100 +295,36 @@
             arrive(("c", "x", r, part), other_core(plane, y, 1 - x, part))
             arrive(("c", "y", r, part), other_core(plane, 1 - y, x, part))
             arrive(("c", "d", r, part), other_core(plane, 1 - y, 1 - x, part))
-    for made in started:
-        made.wait_send()
-    own.wait()
-
-
-COPIES = PARTS * (3 + 3 + 4 + 4 + 14)
-
-
-def gather_all(item_factors, item_count):
-    rows, width = item_factors.shape
-    shard = item_factors.reshape(4, rows // 4, width)
-    return pl.pallas_call(
-        gather_kernel,
-        out_shape=jax.ShapeDtypeStruct((item_count, 4, rows // 4, width), item_factors.dtype),
-        in_specs=[pl.BlockSpec(memory_space=pl.ANY)],
-        out_specs=pl.BlockSpec(memory_space=pl.ANY),
-        scratch_shapes=[
-            pltpu.SemaphoreType.DMA((COPIES,)),
-            pltpu.SemaphoreType.DMA((COPIES,)),
-            pltpu.SemaphoreType.DMA,
-        ],
-        compiler_params=pltpu.CompilerParams(collective_id=0, has_side_effects=True),
-    )(shard)
-
-
-GROUP = 4
-
-
-def solve_kernel(
-    head_ids, tail_ids, start, gram, head_counts, tail_counts, items, out, residual_out, tiles, weights, acc, sem
-):
-    head_count, tail_count = head_counts.shape[0], tail_counts.shape[0]
-    total = head_count + tail_count
-    size, width = tiles.shape[1], tiles.shape[2]
-
-    def fetch(k):
-        block = head_ids[k] if k < head_count else tail_ids[k - head_count]
-        return pltpu.make_async_copy(items.at[block], tiles.at[k], sem.at[k])
-
-    for k in range(total):
-        fetch(k).start()
-    last = (((1,), (1,)), ((), ()))
-
-    def group_tiles(g):
-        return tiles[pl.ds(g * GROUP, GROUP)].reshape(GROUP * size, width)
-
-    def data_part(rounded, rows, weight):
+
+    def each_group(step):
+        for ids, count, base in ((head_ids, heads, 0), (tail_ids, tails, heads // GROUP)):
+
+            def body(g, carry, ids=ids, base=base):
+                rows = jnp.concatenate([items[ids[g * GROUP + k]] for k in range(GROUP)], axis=0)
+                step(base + g, rows)
+                return carry
+
+            lax.fori_loop(0, count // GROUP, body, 0)
+
+    def data_part(rounded, rows, g):
         scores = lax.dot_general(rounded, rows, last, preferred_element_type=jnp.float32)
-        scaled = (scores * weight.astype(jnp.float32)).astype(jnp.bfloat16)
+        scaled = (scores * weights[g].astype(jnp.float32)).astype(jnp.bfloat16)
         return jnp.dot(scaled, rows, preferred_element_type=jnp.float32)
 
-    def dense_part(vector):
-        image = jnp.dot(
-            vector, gram[...], precision=lax.Precision.HIGHEST, preferred_element_type=jnp.float32
-        )
-        return image + ridge_term * vector
-
-    start_vec = start[...]
-    acc[...] = -dense_part(start_vec)
-    rounded_start = start_vec.astype(jnp.bfloat16)
-    for k in range(total):
-        fetch(k).wait()
-
-    def first(counts, base):
-        def body(g, carry):
-            weight_list, rated_list = [], []
-            for k in range(GROUP):
-                count = counts[g * GROUP + k].astype(jnp.float32)
-                weight = conf_alpha * count
-                weight_list.append(weight.astype(jnp.bfloat16))
-                rated_list.append(jnp.where(count > 0, 1.0 + weight, 0.0).astype(jnp.bfloat16))
-            weight = jnp.concatenate(weight_list, axis=1)
-            rated = jnp.concatenate(rated_list, axis=1)
-            weights[base + g] = weight
-            rows = group_tiles(base + g)
-            acc[...] += jnp.dot(rated, rows, preferred_element_type=jnp.float32) - data_part(
-                rounded_start, rows, weight
-            )
-            return carry
-
-        lax.fori_loop(0, counts.shape[0] // GROUP, body, 0)
-
-    first(head_counts, 0)
-    first(tail_counts, head_count // GROUP)
+    def first_step(g, rows):
+        target = jnp.dot(rated[g], rows, preferred_element_type=jnp.float32)
+        acc[...] += target - data_part(rounded_start, rows, g)
+
+    each_group(first_step)
 
     def apply(vector):
         acc[...] = dense_part(vector)
         rounded = vector.astype(jnp.bfloat16)
 
-        def body(g, carry):
-            acc[...] += data_part(rounded, group_tiles(g), weights[g])
-            return carry
-
-        lax.fori_loop(0, total // GROUP, body, 0)
+        def step(g, rows):
+            acc[...] += data_part(rounded, rows, g)
+
+        each_group(step)
         return acc[...]
 
     solution = start_vec
@@ -321,39 +342,47 @@
             norm_now = norm_next
     out[...] = solution
     residual_out[...] = residual
+    for made in started:
+        made.wait_send()
 
 
 def local_gathered(user_factors, item_factors, head_ids, tail_ids, head_counts, tail_counts):
     size, width = head_counts.shape[-1], item_factors.shape[1]
-    items = gather_all(item_factors, lax.axis_size("item"))
-    flat = items.reshape(-1, width)
-    gram_matrix = lax.dot_general(
-        flat, flat, (((0,), (0,)), ((), ())), preferred_element_type=jnp.float32
-    )
-    total = head_counts.shape[1] + tail_counts.shape[1]
+    heads, tails = head_counts.shape[1], tail_counts.shape[1]
+    shard_blocks = item_factors.shape[0] // size
+    groups = (heads + tails) // GROUP
     smem = pl.BlockSpec(memory_space=pltpu.SMEM)
     vmem = pl.BlockSpec(memory_space=pltpu.VMEM)
+    anywhere = pl.BlockSpec(memory_space=pl.ANY)
     shape = jax.ShapeDtypeStruct(user_factors.shape, jnp.float32)
     return pl.pallas_call(
         solve_kernel,
         out_shape=(shape, shape),
-        in_specs=[smem, smem, vmem, vmem, vmem, vmem, pl.BlockSpec(memory_space=pl.ANY)],
+        in_specs=[smem, smem, vmem, anywhere, anywhere, anywhere],
         out_specs=(vmem, vmem),
         scratch_shapes=[
-            pltpu.VMEM((total, size, width), jnp.bfloat16),
-            pltpu.VMEM((total // GROUP, size, GROUP * size), jnp.bfloat16),
+            pltpu.VMEM((lax.axis_size("item") * shard_blocks, size, width), jnp.bfloat16),
+            pltpu.VMEM((heads, size, size), jnp.int32),
+            pltpu.VMEM((tails, size, size), jnp.int32),
+            pltpu.VMEM((groups, size, GROUP * size), jnp.bfloat16),
+            pltpu.VMEM((groups, size, GROUP * size), jnp.bfloat16),
+            pltpu.VMEM((width, width), jnp.float32),
+            pltpu.VMEM((width, width), jnp.float32),
             pltpu.VMEM((size, width), jnp.float32),
-            pltpu.SemaphoreType.DMA((total,)),
+            pltpu.SemaphoreType.DMA((COPIES,)),
+            pltpu.SemaphoreType.DMA((COPIES,)),
+            pltpu.SemaphoreType.DMA((3,)),
         ],
-        compiler_params=pltpu.CompilerParams(vmem_limit_bytes=40 * 1024 * 1024),
+        compiler_params=pltpu.CompilerParams(
+            collective_id=0, has_side_effects=True, vmem_limit_bytes=52 * 1024 * 1024
+        ),
     )(
         head_ids,
         tail_ids.reshape(-1),
         user_factors,
-        gram_matrix,
+        item_factors.reshape(shard_blocks, size, width),
         head_counts[0],
         tail_counts[0],
-        items.reshape(-1, size, width),
     )
 
 

time: 119 us -> 102 us (0.86)
  the two profiles are of different devices: /device:TPU:17 before, /device:TPU:5 now
where the time goes in v2:
time: 102 us
  Pallas kernels  97.9 us (96%)
  local copies, waits for them, and re-layouts  3.66 us (4%)
    pallas_call x1, Pallas kernels, local_gathered(): pl.pallas_call(solve_kernel, out_shape=(shape, shape), in_specs=[smem, sm...  97.9 us
    unnamed x8, local copies, waits for them, and re-layouts  3.66 us

profile of v2, /device:TPU:5, one launch (start us, length us, event | category | flops | bytes accessed | tf_op | source)
XLA Modules:
  0.0 102.2 jit_solution(17828592398632798385)
XLA Ops:
  0.6 0.0 copy-start
  0.6 0.9 copy-done
  1.6 0.0 copy-start.1
  1.6 0.7 copy-done.1
  2.2 0.0 copy-start.2
  2.2 0.7 copy-done.2
  2.9 97.9 %shard_map.77 = (f32[256,256]{1,0:T(8,128)S(1)}, f32[256,256]{1,0:T(8,128)S(1)}) custom-call(s32[8]{0:T(128)S(1)} %copy-done.1, s32[16]{0:T(128)S(1)} %bitcast.4, f32[256,256]{1,0:T(8,128)S(1)} %copy-done, bf16[16,256,256]{2,1,0:T(8,128)(2,1)} %bitcast.6, s32[8,256,256]{2,1,0:T(8,128)} %bitcast.7, s32[16,256,256]{2,1,0:T(8,128)} %bitcast.5), custom_call_target="tpu_custom_call" | custom-call | tf_op jit(solution)/shard_map/pallas_call | solution.py:358
  100.8 0.7 copy.10
  101.5 0.7 copy.11
Async XLA Ops:
  0.6 1.0 copy-start
  1.6 0.7 copy-start.1
  2.2 0.7 copy-start.2

commit v3 on v2

--- a/solution.py
+++ b/solution.py
@@ -108,7 +108,7 @@
 PARTS = 4
 STEPS = (1, 3, 2)
 GROUP = 4
-COPIES = PARTS * (3 + 3 + 4 + 4 + 14) + 1
+COPIES = PARTS * (3 + 3 + 4 + 4 + 14 + 2) + 1
 
 
 def solve_kernel(
@@ -161,12 +161,29 @@
             device_id_type=pl.DeviceIdType.MESH,
         )
 
-    started = []
+    started, started_where = [], []
 
     def send(name, source, target, device):
         made = copy(name, source, target, device)
         made.start()
         started.append(made)
+
+    def send_where(flag, name, source, target, device, via=None):
+        if flag is True:
+            return send(name, source, target, device)
+        made = pltpu.make_async_remote_copy(
+            src_ref=source,
+            dst_ref=target,
+            send_sem=send_sem.at[slot(via or name)],
+            recv_sem=recv_sem.at[slot(name)],
+            device_id=device,
+            device_id_type=pl.DeviceIdType.MESH,
+        )
+        pl.when(flag)(made.start)
+        started_where.append((flag, made))
+
+    def not_near(r):
+        return {1: z == 0, 2: True, 3: z == 3}[r]
 
     def arrive(name, target):
         copy(name, target, target, side_c).wait_recv()
@@ -212,20 +229,20 @@
             send(("y", r, part), here, here, side_y)
             pass_on(("z", r, part), here)
         take(("y", 0, part), place(z, 1 - y, x, part))
-        take(("d", 0, part), place(z, 1 - y, 1 - x, part))
+        corner = place(z, 1 - y, 1 - x, part)
+        arrive(("d", 0, part), corner)
+        send_where(z <= 2, ("d", 1, part), corner, corner, dev(x, y, (z + 1) % 4, c), ("u", part))
+        send_where(z >= 1, ("d", 3, part), corner, corner, dev(x, y, (z + 3) % 4, c), ("v", part))
+        pass_on(("d", 0, part), corner)
 
     def side_part(part):
         for r in STEPS:
             plane = (z + 4 - r) % 4
             from_x, from_y = place(plane, y, 1 - x, part), place(plane, 1 - y, x, part)
-            by_x = r == 1 or (r == 2 and part % 2 == 0) or (r == 3 and part % 2 == 0)
             arrive(("x", r, part), from_x)
-            if not by_x:
-                send(("d", r, part), from_x, from_x, side_y)
             pass_on(("x", r, part), from_x)
             arrive(("y", r, part), from_y)
-            if by_x:
-                send(("d", r, part), from_y, from_y, side_x)
+            send_where(not_near(r), ("d", r, part), from_y, from_y, side_x)
             pass_on(("y", r, part), from_y)
 
     def corner_part(part):
@@ -344,6 +361,8 @@
     residual_out[...] = residual
     for made in started:
         made.wait_send()
+    for flag, made in started_where:
+        pl.when(flag)(made.wait_send)
 
 
 def local_gathered(user_factors, item_factors, head_ids, tail_ids, head_counts, tail_counts):

time: 102 us -> 102 us (level)
  no operation moved by 1% of the time
where the time goes in v3:
time: 102 us
  Pallas kernels  98 us (96%)
  local copies, waits for them, and re-layouts  3.66 us (4%)
    pallas_call x1, Pallas kernels, local_gathered(): pl.pallas_call(solve_kernel, out_shape=(shape, shape), in_specs=[smem, sm...  98 us
    unnamed x8, local copies, waits for them, and re-layouts  3.66 us

profile of v3, /device:TPU:5, one launch (start us, length us, event | category | flops | bytes accessed | tf_op | source)
XLA Modules:
  0.0 102.3 jit_solution(10639027937288833414)
XLA Ops:
  0.6 0.0 copy-start
  0.6 0.9 copy-done
  1.6 0.0 copy-start.1
  1.6 0.7 copy-done.1
  2.2 0.0 copy-start.2
  2.2 0.7 copy-done.2
  2.9 98.0 %shard_map.77 = (f32[256,256]{1,0:T(8,128)S(1)}, f32[256,256]{1,0:T(8,128)S(1)}) custom-call(s32[8]{0:T(128)S(1)} %copy-done.1, s32[16]{0:T(128)S(1)} %bitcast.4, f32[256,256]{1,0:T(8,128)S(1)} %copy-done, bf16[16,256,256]{2,1,0:T(8,128)(2,1)} %bitcast.6, s32[8,256,256]{2,1,0:T(8,128)} %bitcast.7, s32[16,256,256]{2,1,0:T(8,128)} %bitcast.5), custom_call_target="tpu_custom_call" | custom-call | tf_op jit(solution)/shard_map/pallas_call | solution.py:377
  100.9 0.7 copy.10
  101.6 0.7 copy.11
Async XLA Ops:
  0.6 1.0 copy-start
  1.6 0.7 copy-start.1
  2.2 0.7 copy-start.2
